TPU v7x, 32 devices: a whole 2x2x4 slice. The times are simulated.
32 devices in a mesh: groups: 2 (over x), query: 16 (over z, y, core).
Axes of the slice: x: 2, y: 2, z: 4, core: 2. Of those that a mesh axis runs over, the one named last changes fastest.
Arguments:
- tokens: bfloat16 [384, 4096], P(('groups', 'query')), parts along dimension 0, may hold values from -6 to 6
- grad_out: bfloat16 [384, 4096], P(('groups', 'query')), parts along dimension 0, may hold values from -6 to 6
- gate_weight: bfloat16 [4096, 14336], P(None, 'query'), may hold values from -0.09375 to 0.09375
- up_weight: bfloat16 [4096, 14336], P(None, 'query'), may hold values from -0.09375 to 0.09375
- query_left: bfloat16 [16, 4096, 32], P('query'), may hold values from -0.09375 to 0.09375
- query_right: bfloat16 [16, 14336, 32], P('query'), may hold values from -0.09375 to 0.09375
Outputs:
- scores: float32 [384, 16], P(('groups', 'query')), parts along dimension 0
There are 2 independent parts, one for each index of `groups`. A program takes and returns all parts, laid end to end along the dimension named above; an argument that names none is the same for every part. Nothing has to cross between parts.
All inputs are finite; a program needn't handle non-finite values.
Results may differ from a plain program's by a relative error of at most 0.0003.
Values may be sent and summed in bfloat16 or wider, within the bound.
No kernel may reach another device: no remote copies, remote signals or barrier semaphores. Data moves between devices by JAX's collectives and lax.ppermute only.
A program may use at most 128 MiB of HBM per device.

v0:
```python
import jax
import jax.numpy as jnp
from jax import lax
from jax.sharding import PartitionSpec as P

AXIS = "query"
F32 = jnp.float32
BF16 = jnp.bfloat16


def swap(x, bit):
    n = lax.axis_size(AXIS)
    return lax.ppermute(x, AXIS, [(i, i ^ bit) for i in range(n)])


def pick(flag, when_zero, when_one):
    return jnp.where(flag == 0, when_zero, when_one)


def z_order(planes):
    order = [0]
    bit = planes // 2
    while bit >= 1:
        order = order + [k | bit for k in order]
        bit //= 2
    return order


def gather_rows(rows, core, planes):
    half = rows.shape[1] // 2
    mine = pick(core, rows[:, :half], rows[:, half:])
    theirs = pick(core, rows[:, half:], rows[:, :half])
    other = swap(theirs, 1)
    chip = pick(core, jnp.concatenate([mine, other]), jnp.concatenate([other, mine]))
    column = jnp.concatenate([chip if k == 0 else swap(chip, 4 * k) for k in z_order(planes)])
    both = jnp.concatenate([column, swap(column, 2)])
    rest = swap(both, 1)
    return pick(core, jnp.concatenate([both, rest], 1), jnp.concatenate([rest, both], 1))


def body(tokens, grad_out, gate_weight, up_weight, query_left, query_right):
    n = lax.axis_size(AXIS)
    planes = n // 4
    here = lax.axis_index(AXIS)
    core, y, z = (here & 1, here >> 1 & 1, here >> 2)
    rank = query_right.shape[2]
    cols = gate_weight.shape[1]
    blocks = query_right[0].T.reshape(rank, n, cols).transpose(1, 0, 2)
    factors = lax.all_to_all(blocks, AXIS, split_axis=0, concat_axis=0, tiled=True)
    factors = factors.reshape(n // 2, 2, rank, cols)
    keep_factors = pick(core, factors[:, 0], factors[:, 1]).reshape(n // 2 * rank, cols)
    send_factors = pick(core, factors[:, 1], factors[:, 0]).reshape(n // 2 * rank, cols)
    whole = gather_rows(tokens, core, planes)
    grads = gather_rows(grad_out, core, planes)
    gate = jnp.dot(whole, gate_weight, preferred_element_type=F32)
    up = jnp.dot(whole, up_weight, preferred_element_type=F32)
    hidden = jax.nn.silu(gate) * up
    head = lax.reduce_precision(hidden, exponent_bits=8, mantissa_bits=7)
    high = head.astype(BF16)
    low = (hidden - head).astype(BF16)

    def project(with_factors):
        dims = (((1,), (1,)), ((), ()))
        return lax.dot_general(
            high, with_factors, dims, preferred_element_type=F32
        ) + lax.dot_general(low, with_factors, dims, preferred_element_type=F32)

    left = jnp.dot(grads, query_left[0], preferred_element_type=F32)
    right = project(keep_factors) + swap(project(send_factors), 1)
    bit, place = (2, y)
    while bit < n:
        half = right.shape[0] // 2
        right = right[:half] + swap(right[half:], bit)
        other = swap(left[half:], bit)
        left = pick(
            place,
            jnp.concatenate([left[:half], other], 1),
            jnp.concatenate([other, left[:half]], 1),
        )
        bit *= 2
        place = here // bit & 1
    own = tokens.shape[0]
    spread = lax.broadcasted_iota(jnp.int32, (n // 2 * rank, n), 0) // rank * 2 + core
    spread = (spread == lax.broadcasted_iota(jnp.int32, (n // 2 * rank, n), 1)).astype(F32)
    sums = jnp.dot(left * right, spread, precision=lax.Precision.HIGHEST)
    return pick(core, sums[:own], sums[own:]) + swap(pick(core, sums[own:], sums[:own]), 1)


def solution(mesh):
    return jax.shard_map(
        body,
        mesh=mesh,
        in_specs=(
            P(("groups", "query"), None),
            P(("groups", "query"), None),
            P(None, "query"),
            P(None, "query"),
            P("query", None, None),
            P("query", None, None),
        ),
        out_specs=P(("groups", "query"), None),
        check_vma=False,
    )
```

profile of v0, /device:TPU:0, one launch (start us, length us, event | category | flops | bytes accessed | tf_op | source)
XLA Modules:
  0.0 86.0 jit_solution(18113915444369536713)
XLA Ops:
  0.0 1.0 %broadcast_select_fusion.4 = (bf16[12,2048]{1,0:T(8,128)(2,1)S(1)}, bf16[12,2048]{1,0:T(8,128)(2,1)S(1)}) fusion(pred[]{:T(512)S(6)} %eq.10, bf16[12,4096]{1,0:T(8,128)(2,1)} %param.7), kind=kLoop, calls=%fused_computation.37 | loop fusion | flops 49152 | bytes 196609 | tf_op jit(solution)/shard_map/jit(_where)/select_n | solution.py:17
  1.0 0.5 collective-permute-start
  1.5 0.9 %broadcast_select_fusion.2 = (bf16[12,2048]{1,0:T(8,128)(2,1)S(1)}, bf16[12,2048]{1,0:T(8,128)(2,1)S(1)}) fusion(pred[]{:T(512)S(6)} %eq.10, bf16[12,4096]{1,0:T(8,128)(2,1)} %param.6), kind=kLoop, calls=%fused_computation.35 | loop fusion | flops 49152 | bytes 196609 | tf_op jit(solution)/shard_map/jit(_where)/select_n | solution.py:17
  2.4 0.1 collective-permute-start.9
  2.6 4.1 %collective-permute-start.1 = (bf16[24,2048]{1,0:T(8,128)(2,1)S(1)}, bf16[24,2048]{1,0:T(8,128)(2,1)S(1)}, u32[]{:S(2)}, u32[]{:S(2)}) collective-permute-start(bf16[24,2048]{1,0:T(8,128)(2,1)S(1)} %get-tuple-element.6), channel_id=1, source_target_pairs={{0,8},{1,9},{2,10},{3,11},{4,12},{5,13},{6,14},{7,15},{8,0},{9,1},... | collective-permute-start | bytes 294920 | tf_op jit(solution)/shard_map/ppermute | solution.py:13
  6.7 1.6 %collective-permute-start.2 = (bf16[24,2048]{1,0:T(8,128)(2,1)S(1)}, bf16[24,2048]{1,0:T(8,128)(2,1)S(1)}, u32[]{:S(2)}, u32[]{:S(2)}) collective-permute-start(bf16[24,2048]{1,0:T(8,128)(2,1)S(1)} %get-tuple-element.6), channel_id=1, source_target_pairs={{0,4},{1,5},{2,6},{3,7},{4,0},{5,1},{6,2},{7,3},{8,12},{9,13},{10,... | collective-permute-start | bytes 294920 | tf_op jit(solution)/shard_map/ppermute | solution.py:13
  8.3 2.0 %collective-permute-start.10 = (bf16[24,2048]{1,0:T(8,128)(2,1)S(1)}, bf16[24,2048]{1,0:T(8,128)(2,1)S(1)}, u32[]{:S(2)}, u32[]{:S(2)}) collective-permute-start(bf16[24,2048]{1,0:T(8,128)(2,1)S(1)} %get-tuple-element.8), channel_id=1, source_target_pairs={{0,8},{1,9},{2,10},{3,11},{4,12},{5,13},{6,14},{7,15},{8,0},{9,1},... | collective-permute-start | bytes 294920 | tf_op jit(solution)/shard_map/ppermute | solution.py:13
  10.3 2.5 %collective-permute-start.11 = (bf16[24,2048]{1,0:T(8,128)(2,1)S(1)}, bf16[24,2048]{1,0:T(8,128)(2,1)S(1)}, u32[]{:S(2)}, u32[]{:S(2)}) collective-permute-start(bf16[24,2048]{1,0:T(8,128)(2,1)S(1)} %get-tuple-element.8), channel_id=1, source_target_pairs={{0,4},{1,5},{2,6},{3,7},{4,0},{5,1},{6,2},{7,3},{8,12},{9,13},{10,... | collective-permute-start | bytes 294920 | tf_op jit(solution)/shard_map/ppermute | solution.py:13
  12.8 6.2 %collective-permute-start.12 = (bf16[24,2048]{1,0:T(8,128)(2,1)S(1)}, bf16[24,2048]{1,0:T(8,128)(2,1)S(1)}, u32[]{:S(2)}, u32[]{:S(2)}) collective-permute-start(bf16[24,2048]{1,0:T(8,128)(2,1)S(1)} %get-tuple-element.8), channel_id=1, source_target_pairs={{0,12},{1,13},{2,14},{3,15},{4,8},{5,9},{6,10},{7,11},{8,4},{9,5},... | collective-permute-start | bytes 294920 | tf_op jit(solution)/shard_map/ppermute | solution.py:13
  19.0 1.6 %collective-permute-start.4 = (bf16[96,2048]{1,0:T(8,128)(2,1)S(1)}, bf16[96,2048]{1,0:T(8,128)(2,1)S(1)}, u32[]{:S(2)}, u32[]{:S(2)}) collective-permute-start(bf16[96,2048]{1,0:T(8,128)(2,1)S(1)} %pad_maximum_fusion), channel_id=1, source_target_pairs={{0,2},{1,3},{2,0},{3,1},{4,6},{5,7},{6,4},{7,5},{8,10},{9,11},{10,... | collective-permute-start | bytes 1179656 | tf_op jit(solution)/shard_map/ppermute | solution.py:13
  20.6 2.3 %collective-permute-done.10 = bf16[24,2048]{1,0:T(8,128)(2,1)S(1)} collective-permute-done((bf16[24,2048]{1,0:T(8,128)(2,1)S(1)}, bf16[24,2048]{1,0:T(8,128)(2,1)S(1)}, u32[]{:S(2)}, u32[]{:S(2)}) %collective-permute-start.10) | collective-permute-done | bytes 98336 | tf_op jit(solution)/shard_map/ppermute | solution.py:13
  23.0 1.9 %collective-permute-start.13 = (bf16[96,2048]{1,0:T(8,128)(2,1)S(1)}, bf16[96,2048]{1,0:T(8,128)(2,1)S(1)}, u32[]{:S(2)}, u32[]{:S(2)}) collective-permute-start(bf16[96,2048]{1,0:T(8,128)(2,1)S(1)} %pad_maximum_fusion.1), channel_id=1, source_target_pairs={{0,2},{1,3},{2,0},{3,1},{4,6},{5,7},{6,4},{7,5},{8,10},{9,11},{10,... | collective-permute-start | bytes 1179656 | tf_op jit(solution)/shard_map/ppermute | solution.py:13
  24.9 4.9 %collective-permute-done.4 = bf16[96,2048]{1,0:T(8,128)(2,1)S(1)} collective-permute-done((bf16[96,2048]{1,0:T(8,128)(2,1)S(1)}, bf16[96,2048]{1,0:T(8,128)(2,1)S(1)}, u32[]{:S(2)}, u32[]{:S(2)}) %collective-permute-start.4) | collective-permute-done | bytes 393248 | tf_op jit(solution)/shard_map/ppermute | solution.py:13
  29.8 0.1 collective-permute-start.5
  29.9 5.5 %collective-permute-done.13 = bf16[96,2048]{1,0:T(8,128)(2,1)S(1)} collective-permute-done((bf16[96,2048]{1,0:T(8,128)(2,1)S(1)}, bf16[96,2048]{1,0:T(8,128)(2,1)S(1)}, u32[]{:S(2)}, u32[]{:S(2)}) %collective-permute-start.13) | collective-permute-done | bytes 393248 | tf_op jit(solution)/shard_map/ppermute | solution.py:13
  35.4 0.1 collective-permute-start.14
  35.5 0.1 copy.34
  35.6 1.1 %copy.32 = bf16[16,32,896]{2,1,0:T(8,128)(2,1)} copy(bf16[16,32,896]{2,0,1:T(8,128)(2,1)S(1)} %bitcast.23) | data formatting | bytes 1835008 | tf_op jit(solution)/shard_map/transpose | solution.py:48
  36.7 8.1 %all-to-all-start = ((bf16[16,32,896]{2,1,0:T(8,128)(2,1)}), bf16[16,32,896]{2,1,0:T(8,128)(2,1)S(1)}, u32[]{:S(2)}, u32[]{:S(2)}) async-start(bf16[16,32,896]{2,1,0:T(8,128)(2,1)} %copy.32), calls=%async_computation | async-start | bytes 1835008 | tf_op jit(solution)/shard_map/all_to_all | solution.py:49
  44.9 2.0 %fusion = f32[192,32]{0,1:T(8,128)S(1)} fusion(bf16[192,2048]{1,0:T(8,128)(2,1)} %collective-permute-done.5, bf16[192,2048]{1,0:T(8,128)(2,1)S(1)} %constant_dynamic-update-slice_fusion, pred[]{:T(512)S(6)} %eq.10, bf16[1,4096,32]{1,2,0:T(8,128)(2,1)S(1)} %copy-done), kind=kOutput, calls=%fused_computation.1 | convolution fusion | flops 57409536 | bytes 1859585 | tf_op jit(solution)/shard_map/dot_general | solution.py:68
  46.9 0.1 fusion.36
  47.0 1.9 %collective-permute-start.6 = (f32[96,32]{0,1:T(8,128)S(1)}, f32[96,32]{0,1:T(8,128)S(1)}, u32[]{:S(2)}, u32[]{:S(2)}) collective-permute-start(f32[96,32]{0,1:T(8,128)S(1)} %get-tuple-element.18), channel_id=1, source_target_pairs={{0,2},{1,3},{2,0},{3,1},{4,6},{5,7},{6,4},{7,5},{8,10},{9,11},{10,... | collective-permute-start | bytes 36872 | tf_op jit(solution)/shard_map/ppermute | solution.py:13
  48.9 5.2 %fusion.10 = f32[192,896]{1,0:T(8,128)S(1)} fusion(bf16[4096,896]{1,0:T(8,128)(2,1)} %param.8, bf16[192,2048]{1,0:T(8,128)(2,1)S(1)} %collective-permute-done.14, bf16[192,2048]{1,0:T(8,128)(2,1)S(1)} %constant_dynamic-update-slice_fusion.5, pred[]{:T(512)S(6)} %eq.10), kind=kOutput, calls=%fused_computation.21 | convolution fusion | flops 1416364032 | bytes 9601025 | tf_op jit(solution)/shard_map/dot_general | solution.py:55
  54.1 0.1 fusion.35
  54.2 1.9 %collective-permute-start.7 = (f32[48,64]{0,1:T(8,128)S(1)}, f32[48,64]{0,1:T(8,128)S(1)}, u32[]{:S(2)}, u32[]{:S(2)}) collective-permute-start(f32[48,64]{0,1:T(8,128)S(1)} %get-tuple-element.16), channel_id=1, source_target_pairs={{0,4},{1,5},{2,6},{3,7},{4,0},{5,1},{6,2},{7,3},{8,12},{9,13},{10,... | collective-permute-start | bytes 36872 | tf_op jit(solution)/shard_map/ppermute | solution.py:13
  56.1 1.9 %multiply_multiply_fusion = f32[192,896]{1,0:T(8,128)S(1)} fusion(f32[192,896]{1,0:T(8,128)S(1)} %fusion.10, bf16[4096,896]{1,0:T(8,128)(2,1)S(1)} %bitcast.27, bf16[192,2048]{1,0:T(8,128)(2,1)S(1)} %collective-permute-done.14, bf16[192,2048]{1,0:T(8,128)(2,1)S(1)} %constant_dynamic-update-slice_fusion.5, pred[]{:T(512)S(6)} %eq.10), kind=kOutput, calls=%fused_computation.15 | convolution fusion | flops 1417224192 | bytes 10289153 | tf_op jit(solution)/shard_map/dot_general | solution.py:56
  58.0 3.4 %collective-permute-done.7 = f32[48,64]{0,1:T(8,128)S(1)} collective-permute-done((f32[48,64]{0,1:T(8,128)S(1)}, f32[48,64]{0,1:T(8,128)S(1)}, u32[]{:S(2)}, u32[]{:S(2)}) %collective-permute-start.7) | collective-permute-done | bytes 12320 | tf_op jit(solution)/shard_map/ppermute | solution.py:13
  61.5 4.4 %all-to-all-done = bf16[16,32,896]{2,1,0:T(8,128)(2,1)S(1)} async-done(((bf16[16,32,896]{2,1,0:T(8,128)(2,1)}), bf16[16,32,896]{2,1,0:T(8,128)(2,1)S(1)}, u32[]{:S(2)}, u32[]{:S(2)}) %all-to-all-start) | async-done | bytes 917536 | tf_op jit(solution)/shard_map/all_to_all | solution.py:49
  65.9 0.1 broadcast_select_fusion.1
  66.0 0.3 fusion.12
  66.3 0.3 convolution_add_fusion
  66.7 0.2 collective-permute-start.15
  66.9 0.3 fusion.13
  67.2 0.9 %collective-permute-done.15 = f32[192,256]{1,0:T(8,128)S(1)} collective-permute-done((f32[192,256]{1,0:T(8,128)S(1)}, f32[192,256]{1,0:T(8,128)S(1)}, u32[]{:S(2)}, u32[]{:S(2)}) %collective-permute-start.15) | collective-permute-done | bytes 196640 | tf_op jit(solution)/shard_map/ppermute | solution.py:13
  68.2 0.3 fusion.7
  68.5 1.7 %collective-permute-start.16 = (f32[96,256]{1,0:T(8,128)S(1)}, f32[96,256]{1,0:T(8,128)S(1)}, u32[]{:S(2)}, u32[]{:S(2)}) collective-permute-start(f32[96,256]{1,0:T(8,128)S(1)} %slice.100), channel_id=1, source_target_pairs={{0,2},{1,3},{2,0},{3,1},{4,6},{5,7},{6,4},{7,5},{8,10},{9,11},{10,... | collective-permute-start | bytes 294920 | tf_op jit(solution)/shard_map/ppermute | solution.py:13
  70.2 0.1 maximum_select_fusion.10
  70.3 3.2 %collective-permute-done.16 = f32[96,256]{1,0:T(8,128)S(1)} collective-permute-done((f32[96,256]{1,0:T(8,128)S(1)}, f32[96,256]{1,0:T(8,128)S(1)}, u32[]{:S(2)}, u32[]{:S(2)}) %collective-permute-start.16) | collective-permute-done | bytes 98336 | tf_op jit(solution)/shard_map/ppermute | solution.py:13
  73.6 3.0 %collective-permute-start.17 = (f32[48,256]{1,0:T(8,128)S(1)}, f32[48,256]{1,0:T(8,128)S(1)}, u32[]{:S(2)}, u32[]{:S(2)}) collective-permute-start(f32[48,256]{1,0:T(8,128)S(1)} %slice.102), channel_id=1, source_target_pairs={{0,4},{1,5},{2,6},{3,7},{4,0},{5,1},{6,2},{7,3},{8,12},{9,13},{10,... | collective-permute-start | bytes 147464 | tf_op jit(solution)/shard_map/ppermute | solution.py:13
  76.6 1.2 %collective-permute-start.8 = (f32[24,128]{1,0:T(8,128)S(1)}, f32[24,128]{1,0:T(8,128)S(1)}, u32[]{:S(2)}, u32[]{:S(2)}) collective-permute-start(f32[24,128]{1,0:T(8,128)S(1)} %get-tuple-element.20), channel_id=1, source_target_pairs={{0,8},{1,9},{2,10},{3,11},{4,12},{5,13},{6,14},{7,15},{8,0},{9,1},... | collective-permute-start | bytes 36872 | tf_op jit(solution)/shard_map/ppermute | solution.py:13
  77.8 0.9 %collective-permute-done.17 = f32[48,256]{1,0:T(8,128)S(1)} collective-permute-done((f32[48,256]{1,0:T(8,128)S(1)}, f32[48,256]{1,0:T(8,128)S(1)}, u32[]{:S(2)}, u32[]{:S(2)}) %collective-permute-start.17) | collective-permute-done | bytes 49184 | tf_op jit(solution)/shard_map/ppermute | solution.py:13
  78.7 3.2 %collective-permute-start.18 = (f32[24,256]{1,0:T(8,128)S(1)}, f32[24,256]{1,0:T(8,128)S(1)}, u32[]{:S(2)}, u32[]{:S(2)}) collective-permute-start(f32[24,256]{1,0:T(8,128)S(1)} %slice.104), channel_id=1, source_target_pairs={{0,8},{1,9},{2,10},{3,11},{4,12},{5,13},{6,14},{7,15},{8,0},{9,1},... | collective-permute-start | bytes 73736 | tf_op jit(solution)/shard_map/ppermute | solution.py:13
  81.9 1.8 %collective-permute-done.18 = f32[24,256]{1,0:T(8,128)S(1)} collective-permute-done((f32[24,256]{1,0:T(8,128)S(1)}, f32[24,256]{1,0:T(8,128)S(1)}, u32[]{:S(2)}, u32[]{:S(2)}) %collective-permute-start.18) | collective-permute-done | bytes 24608 | tf_op jit(solution)/shard_map/ppermute | solution.py:13
  83.6 0.4 fusion.14
  84.0 0.1 slice_select_fusion
  84.1 1.2 %collective-permute-done.19 = f32[12,16]{0,1:T(8,128)S(1)} collective-permute-done((f32[12,16]{0,1:T(8,128)S(1)}, f32[12,16]{0,1:T(8,128)S(1)}, u32[]{:S(2)}, u32[]{:S(2)}) %collective-permute-start.19) | collective-permute-done | bytes 800 | tf_op jit(solution)/shard_map/ppermute | solution.py:13
  85.3 0.1 select_add_fusion
  85.4 0.7 copy.33
  (45 shorter events, 0.5 us)
Async XLA Ops:
  0.0 44.9 %copy-start = (bf16[1,4096,32]{1,2,0:T(8,128)(2,1)S(1)}, bf16[1,4096,32]{1,2,0:T(8,128)(2,1)}, u32[]{:S(2)}) copy-start(bf16[1,4096,32]{1,2,0:T(8,128)(2,1)} %param.10) | copy-start | bytes 786436
  0.0 35.5 %copy-start.1 = (bf16[1,14336,32]{1,2,0:T(8,128)(2,1)S(1)}, bf16[1,14336,32]{1,2,0:T(8,128)(2,1)}, u32[]{:S(2)}) copy-start(bf16[1,14336,32]{1,2,0:T(8,128)(2,1)} %param.11) | copy-start | bytes 2752516
  1.0 1.5 %collective-permute-start = (bf16[12,2048]{1,0:T(8,128)(2,1)S(1)}, bf16[12,2048]{1,0:T(8,128)(2,1)S(1)}, u32[]{:S(2)}, u32[]{:S(2)}) collective-permute-start(bf16[12,2048]{1,0:T(8,128)(2,1)S(1)} %get-tuple-element.11), channel_id=1, source_target_pairs={{0,1},{1,0},{2,3},{3,2},{4,5},{5,4},{6,7},{7,6},{8,9},{9,8},{10,11... | collective-permute-start | bytes 147464 | tf_op jit(solution)/shard_map/ppermute | solution.py:13
  2.4 5.9 %collective-permute-start.9 = (bf16[12,2048]{1,0:T(8,128)(2,1)S(1)}, bf16[12,2048]{1,0:T(8,128)(2,1)S(1)}, u32[]{:S(2)}, u32[]{:S(2)}) collective-permute-start(bf16[12,2048]{1,0:T(8,128)(2,1)S(1)} %get-tuple-element.13), channel_id=1, source_target_pairs={{0,1},{1,0},{2,3},{3,2},{4,5},{5,4},{6,7},{7,6},{8,9},{9,8},{10,11... | collective-permute-start | bytes 147464 | tf_op jit(solution)/shard_map/ppermute | solution.py:13
  2.6 10.2 %collective-permute-start.1 = (bf16[24,2048]{1,0:T(8,128)(2,1)S(1)}, bf16[24,2048]{1,0:T(8,128)(2,1)S(1)}, u32[]{:S(2)}, u32[]{:S(2)}) collective-permute-start(bf16[24,2048]{1,0:T(8,128)(2,1)S(1)} %get-tuple-element.6), channel_id=1, source_target_pairs={{0,8},{1,9},{2,10},{3,11},{4,12},{5,13},{6,14},{7,15},{8,0},{9,1},... | collective-permute-start | bytes 294920 | tf_op jit(solution)/shard_map/ppermute | solution.py:13
  6.7 12.3 %collective-permute-start.2 = (bf16[24,2048]{1,0:T(8,128)(2,1)S(1)}, bf16[24,2048]{1,0:T(8,128)(2,1)S(1)}, u32[]{:S(2)}, u32[]{:S(2)}) collective-permute-start(bf16[24,2048]{1,0:T(8,128)(2,1)S(1)} %get-tuple-element.6), channel_id=1, source_target_pairs={{0,4},{1,5},{2,6},{3,7},{4,0},{5,1},{6,2},{7,3},{8,12},{9,13},{10,... | collective-permute-start | bytes 294920 | tf_op jit(solution)/shard_map/ppermute | solution.py:13
  8.3 10.7 %collective-permute-start.3 = (bf16[24,2048]{1,0:T(8,128)(2,1)S(1)}, bf16[24,2048]{1,0:T(8,128)(2,1)S(1)}, u32[]{:S(2)}, u32[]{:S(2)}) collective-permute-start(bf16[24,2048]{1,0:T(8,128)(2,1)S(1)} %get-tuple-element.6), channel_id=1, source_target_pairs={{0,12},{1,13},{2,14},{3,15},{4,8},{5,9},{6,10},{7,11},{8,4},{9,5},... | collective-permute-start | bytes 294920 | tf_op jit(solution)/shard_map/ppermute | solution.py:13
  8.3 14.6 %collective-permute-start.10 = (bf16[24,2048]{1,0:T(8,128)(2,1)S(1)}, bf16[24,2048]{1,0:T(8,128)(2,1)S(1)}, u32[]{:S(2)}, u32[]{:S(2)}) collective-permute-start(bf16[24,2048]{1,0:T(8,128)(2,1)S(1)} %get-tuple-element.8), channel_id=1, source_target_pairs={{0,8},{1,9},{2,10},{3,11},{4,12},{5,13},{6,14},{7,15},{8,0},{9,1},... | collective-permute-start | bytes 294920 | tf_op jit(solution)/shard_map/ppermute | solution.py:13
  10.3 12.6 %collective-permute-start.11 = (bf16[24,2048]{1,0:T(8,128)(2,1)S(1)}, bf16[24,2048]{1,0:T(8,128)(2,1)S(1)}, u32[]{:S(2)}, u32[]{:S(2)}) collective-permute-start(bf16[24,2048]{1,0:T(8,128)(2,1)S(1)} %get-tuple-element.8), channel_id=1, source_target_pairs={{0,4},{1,5},{2,6},{3,7},{4,0},{5,1},{6,2},{7,3},{8,12},{9,13},{10,... | collective-permute-start | bytes 294920 | tf_op jit(solution)/shard_map/ppermute | solution.py:13
  12.8 10.2 %collective-permute-start.12 = (bf16[24,2048]{1,0:T(8,128)(2,1)S(1)}, bf16[24,2048]{1,0:T(8,128)(2,1)S(1)}, u32[]{:S(2)}, u32[]{:S(2)}) collective-permute-start(bf16[24,2048]{1,0:T(8,128)(2,1)S(1)} %get-tuple-element.8), channel_id=1, source_target_pairs={{0,12},{1,13},{2,14},{3,15},{4,8},{5,9},{6,10},{7,11},{8,4},{9,5},... | collective-permute-start | bytes 294920 | tf_op jit(solution)/shard_map/ppermute | solution.py:13
  19.0 10.8 %collective-permute-start.4 = (bf16[96,2048]{1,0:T(8,128)(2,1)S(1)}, bf16[96,2048]{1,0:T(8,128)(2,1)S(1)}, u32[]{:S(2)}, u32[]{:S(2)}) collective-permute-start(bf16[96,2048]{1,0:T(8,128)(2,1)S(1)} %pad_maximum_fusion), channel_id=1, source_target_pairs={{0,2},{1,3},{2,0},{3,1},{4,6},{5,7},{6,4},{7,5},{8,10},{9,11},{10,... | collective-permute-start | bytes 1179656 | tf_op jit(solution)/shard_map/ppermute | solution.py:13
  23.0 12.4 %collective-permute-start.13 = (bf16[96,2048]{1,0:T(8,128)(2,1)S(1)}, bf16[96,2048]{1,0:T(8,128)(2,1)S(1)}, u32[]{:S(2)}, u32[]{:S(2)}) collective-permute-start(bf16[96,2048]{1,0:T(8,128)(2,1)S(1)} %pad_maximum_fusion.1), channel_id=1, source_target_pairs={{0,2},{1,3},{2,0},{3,1},{4,6},{5,7},{6,4},{7,5},{8,10},{9,11},{10,... | collective-permute-start | bytes 1179656 | tf_op jit(solution)/shard_map/ppermute | solution.py:13
  29.8 15.1 %collective-permute-start.5 = (bf16[192,2048]{1,0:T(8,128)(2,1)S(1)}, bf16[192,2048]{1,0:T(8,128)(2,1)}, u32[]{:S(2)}, u32[]{:S(2)}) collective-permute-start(bf16[192,2048]{1,0:T(8,128)(2,1)S(1)} %constant_dynamic-update-slice_fusion), channel_id=1, source_target_pairs={{0,1},{1,0},{2,3},{3,2},{4,5},{5,4},{6,7},{7,6},{8,9},{9,8},{10,11... | collective-permute-start | bytes 2359304 | tf_op jit(solution)/shard_map/ppermute | solution.py:13
  35.4 13.5 %collective-permute-start.14 = (bf16[192,2048]{1,0:T(8,128)(2,1)S(1)}, bf16[192,2048]{1,0:T(8,128)(2,1)S(1)}, u32[]{:S(2)}, u32[]{:S(2)}) collective-permute-start(bf16[192,2048]{1,0:T(8,128)(2,1)S(1)} %constant_dynamic-update-slice_fusion.5), channel_id=1, source_target_pairs={{0,1},{1,0},{2,3},{3,2},{4,5},{5,4},{6,7},{7,6},{8,9},{9,8},{10,11... | collective-permute-start | bytes 2359304 | tf_op jit(solution)/shard_map/ppermute | solution.py:13
  36.7 29.2 %all-to-all-start = ((bf16[16,32,896]{2,1,0:T(8,128)(2,1)}), bf16[16,32,896]{2,1,0:T(8,128)(2,1)S(1)}, u32[]{:S(2)}, u32[]{:S(2)}) async-start(bf16[16,32,896]{2,1,0:T(8,128)(2,1)} %copy.32), calls=%async_computation | async-start | bytes 1835008 | tf_op jit(solution)/shard_map/all_to_all | solution.py:49
  47.0 9.1 %slice-start = ((s8[7340032]{0:T(1024)(128)(4,1)}), s8[4194304]{0:T(1024)(128)(4,1)S(1)}, s32[]{:S(2)}) async-start(s8[7340032]{0:T(1024)(128)(4,1)} %bitcast.26), calls=%async_computation.1 | async-start | bytes 8388608
  47.0 9.1 %slice-start.1 = ((s8[7340032]{0:T(1024)(128)(4,1)}), s8[3145728]{0:T(1024)(128)(4,1)S(1)}, s32[]{:S(2)}) async-start(s8[7340032]{0:T(1024)(128)(4,1)} %bitcast.26), calls=%async_computation.2 | async-start | bytes 6291456
  47.0 7.1 %collective-permute-start.6 = (f32[96,32]{0,1:T(8,128)S(1)}, f32[96,32]{0,1:T(8,128)S(1)}, u32[]{:S(2)}, u32[]{:S(2)}) collective-permute-start(f32[96,32]{0,1:T(8,128)S(1)} %get-tuple-element.18), channel_id=1, source_target_pairs={{0,2},{1,3},{2,0},{3,1},{4,6},{5,7},{6,4},{7,5},{8,10},{9,11},{10,... | collective-permute-start | bytes 36872 | tf_op jit(solution)/shard_map/ppermute | solution.py:13
  54.2 7.3 %collective-permute-start.7 = (f32[48,64]{0,1:T(8,128)S(1)}, f32[48,64]{0,1:T(8,128)S(1)}, u32[]{:S(2)}, u32[]{:S(2)}) collective-permute-start(f32[48,64]{0,1:T(8,128)S(1)} %get-tuple-element.16), channel_id=1, source_target_pairs={{0,4},{1,5},{2,6},{3,7},{4,0},{5,1},{6,2},{7,3},{8,12},{9,13},{10,... | collective-permute-start | bytes 36872 | tf_op jit(solution)/shard_map/ppermute | solution.py:13
  66.7 1.5 %collective-permute-start.15 = (f32[192,256]{1,0:T(8,128)S(1)}, f32[192,256]{1,0:T(8,128)S(1)}, u32[]{:S(2)}, u32[]{:S(2)}) collective-permute-start(f32[192,256]{1,0:T(8,128)S(1)} %convolution_add_fusion), channel_id=1, source_target_pairs={{0,1},{1,0},{2,3},{3,2},{4,5},{5,4},{6,7},{7,6},{8,9},{9,8},{10,11... | collective-permute-start | bytes 589832 | tf_op jit(solution)/shard_map/ppermute | solution.py:13
  68.5 5.0 %collective-permute-start.16 = (f32[96,256]{1,0:T(8,128)S(1)}, f32[96,256]{1,0:T(8,128)S(1)}, u32[]{:S(2)}, u32[]{:S(2)}) collective-permute-start(f32[96,256]{1,0:T(8,128)S(1)} %slice.100), channel_id=1, source_target_pairs={{0,2},{1,3},{2,0},{3,1},{4,6},{5,7},{6,4},{7,5},{8,10},{9,11},{10,... | collective-permute-start | bytes 294920 | tf_op jit(solution)/shard_map/ppermute | solution.py:13
  73.6 5.1 %collective-permute-start.17 = (f32[48,256]{1,0:T(8,128)S(1)}, f32[48,256]{1,0:T(8,128)S(1)}, u32[]{:S(2)}, u32[]{:S(2)}) collective-permute-start(f32[48,256]{1,0:T(8,128)S(1)} %slice.102), channel_id=1, source_target_pairs={{0,4},{1,5},{2,6},{3,7},{4,0},{5,1},{6,2},{7,3},{8,12},{9,13},{10,... | collective-permute-start | bytes 147464 | tf_op jit(solution)/shard_map/ppermute | solution.py:13
  76.6 5.3 %collective-permute-start.8 = (f32[24,128]{1,0:T(8,128)S(1)}, f32[24,128]{1,0:T(8,128)S(1)}, u32[]{:S(2)}, u32[]{:S(2)}) collective-permute-start(f32[24,128]{1,0:T(8,128)S(1)} %get-tuple-element.20), channel_id=1, source_target_pairs={{0,8},{1,9},{2,10},{3,11},{4,12},{5,13},{6,14},{7,15},{8,0},{9,1},... | collective-permute-start | bytes 36872 | tf_op jit(solution)/shard_map/ppermute | solution.py:13
  78.7 5.0 %collective-permute-start.18 = (f32[24,256]{1,0:T(8,128)S(1)}, f32[24,256]{1,0:T(8,128)S(1)}, u32[]{:S(2)}, u32[]{:S(2)}) collective-permute-start(f32[24,256]{1,0:T(8,128)S(1)} %slice.104), channel_id=1, source_target_pairs={{0,8},{1,9},{2,10},{3,11},{4,12},{5,13},{6,14},{7,15},{8,0},{9,1},... | collective-permute-start | bytes 73736 | tf_op jit(solution)/shard_map/ppermute | solution.py:13
  84.1 1.2 %collective-permute-start.19 = (f32[12,16]{0,1:T(8,128)S(1)}, f32[12,16]{0,1:T(8,128)S(1)}, u32[]{:S(2)}, u32[]{:S(2)}) collective-permute-start(f32[12,16]{0,1:T(8,128)S(1)} %slice_select_fusion), channel_id=1, source_target_pairs={{0,1},{1,0},{2,3},{3,2},{4,5},{5,4},{6,7},{7,6},{8,9},{9,8},{10,11... | collective-permute-start | bytes 2312 | tf_op jit(solution)/shard_map/ppermute | solution.py:13
where the time goes:
time: 86.3 us; the launch traced here: 86 us
  starting transfers between devices  41.8 us (48%)
  waiting for transfers between devices  28.6 us (33%)
  matrix products  10.7 us (12%)
  other arithmetic  2.38 us (3%)
  local copies, waits for them, and re-layouts  2.3 us (3%)
    ppermute x20, starting transfers between devices, swap(): return lax.ppermute(x, AXIS, [(i, i ^ bit) for i in range(n)])  33.7 us
    ppermute x20, waiting for transfers between devices, swap(): return lax.ppermute(x, AXIS, [(i, i ^ bit) for i in range(n)])  24.2 us
    all_to_all x1, starting transfers between devices, body(): lax.all_to_all(blocks, AXIS, split_axis=0, concat_axis=0, tiled=True)  8.12 us
    dot_general x1, matrix products, body(): gate = jnp.dot(whole, gate_weight, preferred_element_type=F32)  5.16 us
    all_to_all x1, waiting for transfers between devices, body(): lax.all_to_all(blocks, AXIS, split_axis=0, concat_axis=0, tiled=True)  4.41 us
    select_n x6, other arithmetic, pick(): return jnp.where(flag == 0, when_zero, when_one)  2.12 us
    dot_general x1, matrix products, body(): left = jnp.dot(grads, query_left[0], preferred_element_type=F32)  1.97 us
    dot_general x1, matrix products, body(): up = jnp.dot(whole, up_weight, preferred_element_type=F32)  1.87 us
  transfers between devices with their start and end apart: 21, of which 10 were waited for; matrix products, arithmetic and copies ran while one was open for 14% of the time, Pallas kernels for 0%

commit v1 on v0

--- a/solution.py
+++ b/solution.py
@@ -46,7 +46,18 @@
     rank = query_right.shape[2]
     cols = gate_weight.shape[1]
     blocks = query_right[0].T.reshape(rank, n, cols).transpose(1, 0, 2)
-    factors = lax.all_to_all(blocks, AXIS, split_axis=0, concat_axis=0, tiled=True)
+    ways, here_2 = (lax.axis_size(AXIS), lax.axis_index(AXIS))
+    width = blocks.shape[0] // ways
+    dims_2 = list(blocks.shape)
+    dims_2[0] = width
+    height = dims_2[0]
+    dims_2[0] = height * ways
+    factors = jnp.zeros(dims_2, blocks.dtype)
+    for mask in range(ways):
+        part = lax.dynamic_slice_in_dim(blocks, (here_2 ^ mask) * width, width, axis=0)
+        if mask:
+            part = lax.ppermute(part, AXIS, [(d, d ^ mask) for d in range(ways)])
+        factors = lax.dynamic_update_slice_in_dim(factors, part, (here_2 ^ mask) * height, axis=0)
     factors = factors.reshape(n // 2, 2, rank, cols)
     keep_factors = pick(core, factors[:, 0], factors[:, 1]).reshape(n // 2 * rank, cols)
     send_factors = pick(core, factors[:, 1], factors[:, 0]).reshape(n // 2 * rank, cols)

time: 86.3 us -> 100 us (1.16)
  waiting for transfers between devices: 28.6 us -> 37 us
  starting transfers between devices: 41.8 us -> 49.7 us
  matrix products: 10.7 us -> 5.99 us
  local copies, waits for them, and re-layouts: 2.3 us -> 6.2 us
  other arithmetic: 2.38 us -> 0.55 us
    ppermute x0 -> x15, starting transfers between devices: none -> 26.8 us  [body(): part = lax.ppermute(part, AXIS, [(d, d ^ mask) for d in range(ways)])]
    ppermute x20, waiting for transfers between devices: 24.2 us -> 36.7 us  [swap(): return lax.ppermute(x, AXIS, [(i, i ^ bit) for i in range(n)])]
    ppermute x20, starting transfers between devices: 33.7 us -> 22.8 us  [swap(): return lax.ppermute(x, AXIS, [(i, i ^ bit) for i in range(n)])]
    all_to_all x1 -> x0, starting transfers between devices: 8.12 us -> none  [body(): lax.all_to_all(blocks, AXIS, split_axis=0, concat_axis=0, tiled=True)]
    all_to_all x1 -> x0, waiting for transfers between devices: 4.41 us -> none  [body(): lax.all_to_all(blocks, AXIS, split_axis=0, concat_axis=0, tiled=True)]
    dot_general x1, matrix products: 5.16 us -> 1.86 us  [body(): gate = jnp.dot(whole, gate_weight, preferred_element_type=F32)]
    another operation x0 -> x1, local copies, waits for them, and re-layouts: none -> 2.67 us
    unnamed x15 -> x36, local copies, waits for them, and re-layouts: 0.16 us -> 2.18 us
  transfers between devices with their start and end apart: 21 -> 35, of which waited for: 10 -> 13; matrix products, arithmetic and copies ran while one was open for 14% -> 7% of each run, Pallas kernels for 0% -> 0%
where the time goes in v1:
time: 100 us
  starting transfers between devices  49.7 us (50%)
  waiting for transfers between devices  37 us (37%)
  local copies, waits for them, and re-layouts  6.2 us (6%)
  matrix products  5.99 us (6%)
    ppermute x20, waiting for transfers between devices, swap(): return lax.ppermute(x, AXIS, [(i, i ^ bit) for i in range(n)])  36.7 us
    ppermute x15, starting transfers between devices, body(): part = lax.ppermute(part, AXIS, [(d, d ^ mask) for d in range(ways)])  26.8 us
    ppermute x20, starting transfers between devices, swap(): return lax.ppermute(x, AXIS, [(i, i ^ bit) for i in range(n)])  22.8 us
    another operation x1, local copies, waits for them, and re-layouts  2.67 us
    unnamed x36, local copies, waits for them, and re-layouts  2.18 us
  transfers between devices with their start and end apart: 35, of which 13 were waited for; matrix products, arithmetic and copies ran while one was open for 7% of the time, Pallas kernels for 0%

profile of v1, /device:TPU:0, one launch (start us, length us, event | category | flops | bytes accessed | tf_op | source)
XLA Modules:
  0.0 100.1 jit_solution(17699926253830695859)
XLA Ops:
  0.0 1.3 %copy.43 = bf16[4,8,16,896]{3,2,1,0:T(8,128)(2,1)S(1)} copy(bf16[4,8,16,896]{3,1,2,0:T(8,128)(2,1)} %bitcast.70) | data formatting | bytes 1835008
  1.4 2.7 %constant_dynamic-slice_fusion = (bf16[32,1,896]{2,1,0:T(2,128)(2,1)S(1)}, bf16[32,1,896]{2,1,0:T(2,128)(2,1)S(1)}, bf16[32,1,896]{2,1,0:T(2,128)(2,1)S(1)}, bf1...) fusion(bf16[32,16,896]{2,1,0:T(8,128)(2,1)S(1)} %bitcast.64, ...), kind=kLoop, calls=%fused_computation.79 | loop fusion | bytes 1835072 | tf_op jit(solution)/shard_map/dynamic-slice.15
  4.1 0.6 copy.74
  4.7 0.5 collective-permute-start.15
  5.2 2.6 %collective-permute-start.16 = (bf16[1,32,896]{2,1,0:T(8,128)(2,1)S(1)}, bf16[1,32,896]{2,1,0:T(8,128)(2,1)S(1)}, u32[]{:S(2)}, u32[]{:S(2)}) collective-permute-start(bf16[1,32,896]{2,1,0:T(8,128)(2,1)S(1)} %bitcast.82), channel_id=1, source_target_pairs={{0,2},{1,3},{2,0},{3,1},{4,6},{5,7},{6,4},{7,5},{8,10},{9,11},{10,... | collective-permute-start | bytes 172040 | tf_op jit(solution)/shard_map/ppermute | solution.py:59
  7.8 0.2 collective-permute-start.17
  8.0 1.8 %collective-permute-start.18 = (bf16[1,32,896]{2,1,0:T(8,128)(2,1)S(1)}, bf16[1,32,896]{2,1,0:T(8,128)(2,1)S(1)}, u32[]{:S(2)}, u32[]{:S(2)}) collective-permute-start(bf16[1,32,896]{2,1,0:T(8,128)(2,1)S(1)} %bitcast.79), channel_id=1, source_target_pairs={{0,4},{1,5},{2,6},{3,7},{4,0},{5,1},{6,2},{7,3},{8,12},{9,13},{10,... | collective-permute-start | bytes 172040 | tf_op jit(solution)/shard_map/ppermute | solution.py:59
  10.3 0.9 collective-permute-done.9
  11.4 1.0 %collective-permute-done = bf16[12,2048]{1,0:T(8,128)(2,1)S(1)} collective-permute-done((bf16[12,2048]{1,0:T(8,128)(2,1)S(1)}, bf16[12,2048]{1,0:T(8,128)(2,1)S(1)}, u32[]{:S(2)}, u32[]{:S(2)}) %collective-permute-start) | collective-permute-done | bytes 49184 | tf_op jit(solution)/shard_map/ppermute | solution.py:13
  12.5 2.8 %collective-permute-start.20 = (bf16[1,32,896]{2,1,0:T(8,128)(2,1)S(1)}, bf16[1,32,896]{2,1,0:T(8,128)(2,1)S(1)}, u32[]{:S(2)}, u32[]{:S(2)}) collective-permute-start(bf16[1,32,896]{2,1,0:T(8,128)(2,1)S(1)} %bitcast.83), channel_id=1, source_target_pairs={{0,6},{1,7},{2,4},{3,5},{4,2},{5,3},{6,0},{7,1},{8,14},{9,15},{10,... | collective-permute-start | bytes 172040 | tf_op jit(solution)/shard_map/ppermute | solution.py:59
  15.5 2.7 %collective-permute-start.22 = (bf16[1,32,896]{2,1,0:T(8,128)(2,1)S(1)}, bf16[1,32,896]{2,1,0:T(8,128)(2,1)S(1)}, u32[]{:S(2)}, u32[]{:S(2)}) collective-permute-start(bf16[1,32,896]{2,1,0:T(8,128)(2,1)S(1)} %bitcast.78), channel_id=1, source_target_pairs={{0,8},{1,9},{2,10},{3,11},{4,12},{5,13},{6,14},{7,15},{8,0},{9,1},... | collective-permute-start | bytes 172040 | tf_op jit(solution)/shard_map/ppermute | solution.py:59
  18.3 3.6 %collective-permute-start.24 = (bf16[1,32,896]{2,1,0:T(8,128)(2,1)S(1)}, bf16[1,32,896]{2,1,0:T(8,128)(2,1)S(1)}, u32[]{:S(2)}, u32[]{:S(2)}) collective-permute-start(bf16[1,32,896]{2,1,0:T(8,128)(2,1)S(1)} %bitcast.76), channel_id=1, source_target_pairs={{0,10},{1,11},{2,8},{3,9},{4,14},{5,15},{6,12},{7,13},{8,2},{9,3},... | collective-permute-start | bytes 172040 | tf_op jit(solution)/shard_map/ppermute | solution.py:59
  22.1 3.6 %collective-permute-start.26 = (bf16[1,32,896]{2,1,0:T(8,128)(2,1)S(1)}, bf16[1,32,896]{2,1,0:T(8,128)(2,1)S(1)}, u32[]{:S(2)}, u32[]{:S(2)}) collective-permute-start(bf16[1,32,896]{2,1,0:T(8,128)(2,1)S(1)} %bitcast.74), channel_id=1, source_target_pairs={{0,12},{1,13},{2,14},{3,15},{4,8},{5,9},{6,10},{7,11},{8,4},{9,5},... | collective-permute-start | bytes 172040 | tf_op jit(solution)/shard_map/ppermute | solution.py:59
  25.7 0.6 collective-permute-start.27
  26.5 4.8 %collective-permute-start.28 = (bf16[1,32,896]{2,1,0:T(8,128)(2,1)S(1)}, bf16[1,32,896]{2,1,0:T(8,128)(2,1)S(1)}, u32[]{:S(2)}, u32[]{:S(2)}) collective-permute-start(bf16[1,32,896]{2,1,0:T(8,128)(2,1)S(1)} %bitcast.72), channel_id=1, source_target_pairs={{0,14},{1,15},{2,12},{3,13},{4,10},{5,11},{6,8},{7,9},{8,6},{9,7},... | collective-permute-start | bytes 172040 | tf_op jit(solution)/shard_map/ppermute | solution.py:59
  31.3 3.3 %collective-permute-start.29 = (bf16[1,32,896]{2,1,0:T(8,128)(2,1)S(1)}, bf16[1,32,896]{2,1,0:T(8,128)(2,1)S(1)}, u32[]{:S(2)}, u32[]{:S(2)}) collective-permute-start(bf16[1,32,896]{2,1,0:T(8,128)(2,1)S(1)} %bitcast.71), channel_id=1, source_target_pairs={{0,15},{1,14},{2,13},{3,12},{4,11},{5,10},{6,9},{7,8},{8,7},{9,6},... | collective-permute-start | bytes 172040 | tf_op jit(solution)/shard_map/ppermute | solution.py:59
  34.6 0.2 collective-permute-done.25
  34.8 0.8 collective-permute-start.11
  35.6 3.8 %collective-permute-start.12 = (bf16[24,2048]{1,0:T(8,128)(2,1)S(1)}, bf16[24,2048]{1,0:T(8,128)(2,1)S(1)}, u32[]{:S(2)}, u32[]{:S(2)}) collective-permute-start(bf16[24,2048]{1,0:T(8,128)(2,1)S(1)} %get-tuple-element.8), channel_id=1, source_target_pairs={{0,12},{1,13},{2,14},{3,15},{4,8},{5,9},{6,10},{7,11},{8,4},{9,5},... | collective-permute-start | bytes 294920 | tf_op jit(solution)/shard_map/ppermute | solution.py:13
  39.4 4.2 %collective-permute-start.1 = (bf16[24,2048]{1,0:T(8,128)(2,1)S(1)}, bf16[24,2048]{1,0:T(8,128)(2,1)S(1)}, u32[]{:S(2)}, u32[]{:S(2)}) collective-permute-start(bf16[24,2048]{1,0:T(8,128)(2,1)S(1)} %get-tuple-element.6), channel_id=1, source_target_pairs={{0,8},{1,9},{2,10},{3,11},{4,12},{5,13},{6,14},{7,15},{8,0},{9,1},... | collective-permute-start | bytes 294920 | tf_op jit(solution)/shard_map/ppermute | solution.py:13
  43.6 4.8 %collective-permute-done.10 = bf16[24,2048]{1,0:T(8,128)(2,1)S(1)} collective-permute-done((bf16[24,2048]{1,0:T(8,128)(2,1)S(1)}, bf16[24,2048]{1,0:T(8,128)(2,1)S(1)}, u32[]{:S(2)}, u32[]{:S(2)}) %collective-permute-start.10) | collective-permute-done | bytes 98336 | tf_op jit(solution)/shard_map/ppermute | solution.py:13
  48.5 2.6 %collective-permute-start.3 = (bf16[24,2048]{1,0:T(8,128)(2,1)S(1)}, bf16[24,2048]{1,0:T(8,128)(2,1)S(1)}, u32[]{:S(2)}, u32[]{:S(2)}) collective-permute-start(bf16[24,2048]{1,0:T(8,128)(2,1)S(1)} %get-tuple-element.6), channel_id=1, source_target_pairs={{0,12},{1,13},{2,14},{3,15},{4,8},{5,9},{6,10},{7,11},{8,4},{9,5},... | collective-permute-start | bytes 294920 | tf_op jit(solution)/shard_map/ppermute | solution.py:13
  51.2 1.6 %collective-permute-start.13 = (bf16[96,2048]{1,0:T(8,128)(2,1)S(1)}, bf16[96,2048]{1,0:T(8,128)(2,1)S(1)}, u32[]{:S(2)}, u32[]{:S(2)}) collective-permute-start(bf16[96,2048]{1,0:T(8,128)(2,1)S(1)} %pad_maximum_fusion.1), channel_id=1, source_target_pairs={{0,2},{1,3},{2,0},{3,1},{4,6},{5,7},{6,4},{7,5},{8,10},{9,11},{10,... | collective-permute-start | bytes 1179656 | tf_op jit(solution)/shard_map/ppermute | solution.py:13
  52.8 4.1 %collective-permute-done.2 = bf16[24,2048]{1,0:T(8,128)(2,1)S(1)} collective-permute-done((bf16[24,2048]{1,0:T(8,128)(2,1)S(1)}, bf16[24,2048]{1,0:T(8,128)(2,1)S(1)}, u32[]{:S(2)}, u32[]{:S(2)}) %collective-permute-start.2) | collective-permute-done | bytes 98336 | tf_op jit(solution)/shard_map/ppermute | solution.py:13
  56.9 1.6 %collective-permute-start.4 = (bf16[96,2048]{1,0:T(8,128)(2,1)S(1)}, bf16[96,2048]{1,0:T(8,128)(2,1)S(1)}, u32[]{:S(2)}, u32[]{:S(2)}) collective-permute-start(bf16[96,2048]{1,0:T(8,128)(2,1)S(1)} %pad_maximum_fusion), channel_id=1, source_target_pairs={{0,2},{1,3},{2,0},{3,1},{4,6},{5,7},{6,4},{7,5},{8,10},{9,11},{10,... | collective-permute-start | bytes 1179656 | tf_op jit(solution)/shard_map/ppermute | solution.py:13
  58.6 11.8 %collective-permute-done.4 = bf16[96,2048]{1,0:T(8,128)(2,1)S(1)} collective-permute-done((bf16[96,2048]{1,0:T(8,128)(2,1)S(1)}, bf16[96,2048]{1,0:T(8,128)(2,1)S(1)}, u32[]{:S(2)}, u32[]{:S(2)}) %collective-permute-start.4) | collective-permute-done | bytes 393248 | tf_op jit(solution)/shard_map/ppermute | solution.py:13
  70.6 0.5 collective-permute-start.14
  71.3 1.5 %collective-permute-done.5 = bf16[192,2048]{1,0:T(8,128)(2,1)S(1)} collective-permute-done((bf16[192,2048]{1,0:T(8,128)(2,1)S(1)}, bf16[192,2048]{1,0:T(8,128)(2,1)S(1)}, u32[]{:S(2)}, u32[]{:S(2)}) %collective-permute-start.5) | collective-permute-done | bytes 786464 | tf_op jit(solution)/shard_map/ppermute | solution.py:13
  72.8 0.6 fusion
  73.5 1.5 %collective-permute-start.6 = (f32[96,32]{0,1:T(8,128)S(1)}, f32[96,32]{0,1:T(8,128)S(1)}, u32[]{:S(2)}, u32[]{:S(2)}) collective-permute-start(f32[96,32]{0,1:T(8,128)S(1)} %get-tuple-element.34), channel_id=1, source_target_pairs={{0,2},{1,3},{2,0},{3,1},{4,6},{5,7},{6,4},{7,5},{8,10},{9,11},{10,... | collective-permute-start | bytes 36872 | tf_op jit(solution)/shard_map/ppermute | solution.py:13
  75.1 1.9 %fusion.10 = f32[192,896]{1,0:T(8,128)S(1)} fusion(bf16[4096,896]{1,0:T(8,128)(2,1)S(1)} %bitcast.86, bf16[192,2048]{1,0:T(8,128)(2,1)S(1)} %collective-permute-done.14, bf16[192,2048]{1,0:T(8,128)(2,1)S(1)} %constant_dynamic-update-slice_fusion.5, pred[]{:T(512)S(6)} %eq.10), kind=kOutput, calls=%fused_computation.21 | convolution fusion | flops 1416364032 | bytes 9601025 | tf_op jit(solution)/shard_map/dot_general | solution.py:66
  77.0 1.9 %multiply_multiply_fusion = f32[192,896]{1,0:T(8,128)S(1)} fusion(f32[192,896]{1,0:T(8,128)S(1)} %fusion.10, bf16[4096,896]{1,0:T(8,128)(2,1)S(1)} %bitcast.88, bf16[192,2048]{1,0:T(8,128)(2,1)S(1)} %collective-permute-done.14, bf16[192,2048]{1,0:T(8,128)(2,1)S(1)} %constant_dynamic-update-slice_fusion.5, pred[]{:T(512)S(6)} %eq.10), kind=kOutput, calls=%fused_computation.15 | convolution fusion | flops 1417224192 | bytes 10289153 | tf_op jit(solution)/shard_map/dot_general | solution.py:67
  78.8 0.3 fusion.12
  79.2 0.3 convolution_add_fusion
  79.7 0.9 collective-permute-start.7
  80.5 0.3 fusion.13
  80.9 2.7 %collective-permute-done.7 = f32[48,64]{0,1:T(8,128)S(1)} collective-permute-done((f32[48,64]{0,1:T(8,128)S(1)}, f32[48,64]{0,1:T(8,128)S(1)}, u32[]{:S(2)}, u32[]{:S(2)}) %collective-permute-start.7) | collective-permute-done | bytes 12320 | tf_op jit(solution)/shard_map/ppermute | solution.py:13
  83.7 0.3 fusion.7
  84.0 1.4 %collective-permute-start.31 = (f32[96,256]{1,0:T(8,128)S(1)}, f32[96,256]{1,0:T(8,128)S(1)}, u32[]{:S(2)}, u32[]{:S(2)}) collective-permute-start(f32[96,256]{1,0:T(8,128)S(1)} %slice.100), channel_id=1, source_target_pairs={{0,2},{1,3},{2,0},{3,1},{4,6},{5,7},{6,4},{7,5},{8,10},{9,11},{10,... | collective-permute-start | bytes 294920 | tf_op jit(solution)/shard_map/ppermute | solution.py:13
  85.5 3.2 %collective-permute-done.31 = f32[96,256]{1,0:T(8,128)S(1)} collective-permute-done((f32[96,256]{1,0:T(8,128)S(1)}, f32[96,256]{1,0:T(8,128)S(1)}, u32[]{:S(2)}, u32[]{:S(2)}) %collective-permute-start.31) | collective-permute-done | bytes 98336 | tf_op jit(solution)/shard_map/ppermute | solution.py:13
  88.7 0.9 collective-permute-start.32
  89.6 0.9 collective-permute-start.8
  90.6 2.3 %collective-permute-done.32 = f32[48,256]{1,0:T(8,128)S(1)} collective-permute-done((f32[48,256]{1,0:T(8,128)S(1)}, f32[48,256]{1,0:T(8,128)S(1)}, u32[]{:S(2)}, u32[]{:S(2)}) %collective-permute-start.32) | collective-permute-done | bytes 49184 | tf_op jit(solution)/shard_map/ppermute | solution.py:13
  92.9 1.7 %collective-permute-start.33 = (f32[24,256]{1,0:T(8,128)S(1)}, f32[24,256]{1,0:T(8,128)S(1)}, u32[]{:S(2)}, u32[]{:S(2)}) collective-permute-start(f32[24,256]{1,0:T(8,128)S(1)} %slice.104), channel_id=1, source_target_pairs={{0,8},{1,9},{2,10},{3,11},{4,12},{5,13},{6,14},{7,15},{8,0},{9,1},... | collective-permute-start | bytes 73736 | tf_op jit(solution)/shard_map/ppermute | solution.py:13
  94.6 3.1 %collective-permute-done.33 = f32[24,256]{1,0:T(8,128)S(1)} collective-permute-done((f32[24,256]{1,0:T(8,128)S(1)}, f32[24,256]{1,0:T(8,128)S(1)}, u32[]{:S(2)}, u32[]{:S(2)}) %collective-permute-start.33) | collective-permute-done | bytes 24608 | tf_op jit(solution)/shard_map/ppermute | solution.py:13
  97.7 0.4 fusion.14
  98.2 1.2 %collective-permute-done.34 = f32[12,16]{0,1:T(8,128)S(1)} collective-permute-done((f32[12,16]{0,1:T(8,128)S(1)}, f32[12,16]{0,1:T(8,128)S(1)}, u32[]{:S(2)}, u32[]{:S(2)}) %collective-permute-start.34) | collective-permute-done | bytes 800 | tf_op jit(solution)/shard_map/ppermute | solution.py:13
  99.4 0.7 copy.26
  (112 shorter events, 2.3 us)
Async XLA Ops:
  0.0 72.8 %copy-start = (bf16[1,4096,32]{1,2,0:T(8,128)(2,1)S(1)}, bf16[1,4096,32]{1,2,0:T(8,128)(2,1)}, u32[]{:S(2)}) copy-start(bf16[1,4096,32]{1,2,0:T(8,128)(2,1)} %param.10) | copy-start | bytes 786436
  0.0 9.9 %copy-start.1 = (bf16[12,4096]{1,0:T(8,128)(2,1)S(1)}, bf16[12,4096]{1,0:T(8,128)(2,1)}, u32[]{:S(2)}) copy-start(bf16[12,4096]{1,0:T(8,128)(2,1)} %param.6) | copy-start | bytes 294916
  0.0 10.0 %copy-start.2 = (bf16[12,4096]{1,0:T(8,128)(2,1)S(1)}, bf16[12,4096]{1,0:T(8,128)(2,1)}, u32[]{:S(2)}) copy-start(bf16[12,4096]{1,0:T(8,128)(2,1)} %param.7) | copy-start | bytes 294916
  4.7 7.8 %collective-permute-start.15 = (bf16[1,32,896]{2,1,0:T(8,128)(2,1)}, bf16[1,32,896]{2,1,0:T(8,128)(2,1)S(1)}, u32[]{:S(2)}, u32[]{:S(2)}) collective-permute-start(bf16[1,32,896]{2,1,0:T(8,128)(2,1)} %bitcast.63), channel_id=1, source_target_pairs={{0,1},{1,0},{2,3},{3,2},{4,5},{5,4},{6,7},{7,6},{8,9},{9,8},{10,11... | collective-permute-start | bytes 172040 | tf_op jit(solution)/shard_map/ppermute | solution.py:59
  5.2 10.1 %collective-permute-start.16 = (bf16[1,32,896]{2,1,0:T(8,128)(2,1)S(1)}, bf16[1,32,896]{2,1,0:T(8,128)(2,1)S(1)}, u32[]{:S(2)}, u32[]{:S(2)}) collective-permute-start(bf16[1,32,896]{2,1,0:T(8,128)(2,1)S(1)} %bitcast.82), channel_id=1, source_target_pairs={{0,2},{1,3},{2,0},{3,1},{4,6},{5,7},{6,4},{7,5},{8,10},{9,11},{10,... | collective-permute-start | bytes 172040 | tf_op jit(solution)/shard_map/ppermute | solution.py:59
  7.8 7.7 %collective-permute-start.17 = (bf16[1,32,896]{2,1,0:T(8,128)(2,1)S(1)}, bf16[1,32,896]{2,1,0:T(8,128)(2,1)S(1)}, u32[]{:S(2)}, u32[]{:S(2)}) collective-permute-start(bf16[1,32,896]{2,1,0:T(8,128)(2,1)S(1)} %bitcast.81), channel_id=1, source_target_pairs={{0,3},{1,2},{2,1},{3,0},{4,7},{5,6},{6,5},{7,4},{8,11},{9,10},{10,... | collective-permute-start | bytes 172040 | tf_op jit(solution)/shard_map/ppermute | solution.py:59
  8.0 10.2 %collective-permute-start.18 = (bf16[1,32,896]{2,1,0:T(8,128)(2,1)S(1)}, bf16[1,32,896]{2,1,0:T(8,128)(2,1)S(1)}, u32[]{:S(2)}, u32[]{:S(2)}) collective-permute-start(bf16[1,32,896]{2,1,0:T(8,128)(2,1)S(1)} %bitcast.79), channel_id=1, source_target_pairs={{0,4},{1,5},{2,6},{3,7},{4,0},{5,1},{6,2},{7,3},{8,12},{9,13},{10,... | collective-permute-start | bytes 172040 | tf_op jit(solution)/shard_map/ppermute | solution.py:59
  9.9 1.3 %collective-permute-start.9 = (bf16[12,2048]{1,0:T(8,128)(2,1)S(1)}, bf16[12,2048]{1,0:T(8,128)(2,1)S(1)}, u32[]{:S(2)}, u32[]{:S(2)}) collective-permute-start(bf16[12,2048]{1,0:T(8,128)(2,1)S(1)} %get-tuple-element.29), channel_id=1, source_target_pairs={{0,1},{1,0},{2,3},{3,2},{4,5},{5,4},{6,7},{7,6},{8,9},{9,8},{10,11... | collective-permute-start | bytes 147464 | tf_op jit(solution)/shard_map/ppermute | solution.py:13
  11.2 1.3 %collective-permute-start = (bf16[12,2048]{1,0:T(8,128)(2,1)S(1)}, bf16[12,2048]{1,0:T(8,128)(2,1)S(1)}, u32[]{:S(2)}, u32[]{:S(2)}) collective-permute-start(bf16[12,2048]{1,0:T(8,128)(2,1)S(1)} %get-tuple-element.27), channel_id=1, source_target_pairs={{0,1},{1,0},{2,3},{3,2},{4,5},{5,4},{6,7},{7,6},{8,9},{9,8},{10,11... | collective-permute-start | bytes 147464 | tf_op jit(solution)/shard_map/ppermute | solution.py:13
  12.5 5.9 %collective-permute-start.19 = (bf16[1,32,896]{2,1,0:T(8,128)(2,1)S(1)}, bf16[1,32,896]{2,1,0:T(8,128)(2,1)S(1)}, u32[]{:S(2)}, u32[]{:S(2)}) collective-permute-start(bf16[1,32,896]{2,1,0:T(8,128)(2,1)S(1)} %bitcast.84), channel_id=1, source_target_pairs={{0,5},{1,4},{2,7},{3,6},{4,1},{5,0},{6,3},{7,2},{8,13},{9,12},{10,... | collective-permute-start | bytes 172040 | tf_op jit(solution)/shard_map/ppermute | solution.py:59
  12.5 9.5 %collective-permute-start.20 = (bf16[1,32,896]{2,1,0:T(8,128)(2,1)S(1)}, bf16[1,32,896]{2,1,0:T(8,128)(2,1)S(1)}, u32[]{:S(2)}, u32[]{:S(2)}) collective-permute-start(bf16[1,32,896]{2,1,0:T(8,128)(2,1)S(1)} %bitcast.83), channel_id=1, source_target_pairs={{0,6},{1,7},{2,4},{3,5},{4,2},{5,3},{6,0},{7,1},{8,14},{9,15},{10,... | collective-permute-start | bytes 172040 | tf_op jit(solution)/shard_map/ppermute | solution.py:59
  15.4 6.8 %collective-permute-start.21 = (bf16[1,32,896]{2,1,0:T(8,128)(2,1)S(1)}, bf16[1,32,896]{2,1,0:T(8,128)(2,1)S(1)}, u32[]{:S(2)}, u32[]{:S(2)}) collective-permute-start(bf16[1,32,896]{2,1,0:T(8,128)(2,1)S(1)} %bitcast.80), channel_id=1, source_target_pairs={{0,7},{1,6},{2,5},{3,4},{4,3},{5,2},{6,1},{7,0},{8,15},{9,14},{10,... | collective-permute-start | bytes 172040 | tf_op jit(solution)/shard_map/ppermute | solution.py:59
  15.5 10.3 %collective-permute-start.22 = (bf16[1,32,896]{2,1,0:T(8,128)(2,1)S(1)}, bf16[1,32,896]{2,1,0:T(8,128)(2,1)S(1)}, u32[]{:S(2)}, u32[]{:S(2)}) collective-permute-start(bf16[1,32,896]{2,1,0:T(8,128)(2,1)S(1)} %bitcast.78), channel_id=1, source_target_pairs={{0,8},{1,9},{2,10},{3,11},{4,12},{5,13},{6,14},{7,15},{8,0},{9,1},... | collective-permute-start | bytes 172040 | tf_op jit(solution)/shard_map/ppermute | solution.py:59
  18.2 8.3 %collective-permute-start.23 = (bf16[1,32,896]{2,1,0:T(8,128)(2,1)S(1)}, bf16[1,32,896]{2,1,0:T(8,128)(2,1)S(1)}, u32[]{:S(2)}, u32[]{:S(2)}) collective-permute-start(bf16[1,32,896]{2,1,0:T(8,128)(2,1)S(1)} %bitcast.77), channel_id=1, source_target_pairs={{0,9},{1,8},{2,11},{3,10},{4,13},{5,12},{6,15},{7,14},{8,1},{9,0},... | collective-permute-start | bytes 172040 | tf_op jit(solution)/shard_map/ppermute | solution.py:59
  18.3 13.0 %collective-permute-start.24 = (bf16[1,32,896]{2,1,0:T(8,128)(2,1)S(1)}, bf16[1,32,896]{2,1,0:T(8,128)(2,1)S(1)}, u32[]{:S(2)}, u32[]{:S(2)}) collective-permute-start(bf16[1,32,896]{2,1,0:T(8,128)(2,1)S(1)} %bitcast.76), channel_id=1, source_target_pairs={{0,10},{1,11},{2,8},{3,9},{4,14},{5,15},{6,12},{7,13},{8,2},{9,3},... | collective-permute-start | bytes 172040 | tf_op jit(solution)/shard_map/ppermute | solution.py:59
  22.0 12.8 %collective-permute-start.25 = (bf16[1,32,896]{2,1,0:T(8,128)(2,1)S(1)}, bf16[1,32,896]{2,1,0:T(8,128)(2,1)S(1)}, u32[]{:S(2)}, u32[]{:S(2)}) collective-permute-start(bf16[1,32,896]{2,1,0:T(8,128)(2,1)S(1)} %bitcast.75), channel_id=1, source_target_pairs={{0,11},{1,10},{2,9},{3,8},{4,15},{5,14},{6,13},{7,12},{8,3},{9,2},... | collective-permute-start | bytes 172040 | tf_op jit(solution)/shard_map/ppermute | solution.py:59
  22.1 12.7 %collective-permute-start.26 = (bf16[1,32,896]{2,1,0:T(8,128)(2,1)S(1)}, bf16[1,32,896]{2,1,0:T(8,128)(2,1)S(1)}, u32[]{:S(2)}, u32[]{:S(2)}) collective-permute-start(bf16[1,32,896]{2,1,0:T(8,128)(2,1)S(1)} %bitcast.74), channel_id=1, source_target_pairs={{0,12},{1,13},{2,14},{3,15},{4,8},{5,9},{6,10},{7,11},{8,4},{9,5},... | collective-permute-start | bytes 172040 | tf_op jit(solution)/shard_map/ppermute | solution.py:59
  25.7 9.9 %collective-permute-start.27 = (bf16[1,32,896]{2,1,0:T(8,128)(2,1)S(1)}, bf16[1,32,896]{2,1,0:T(8,128)(2,1)S(1)}, u32[]{:S(2)}, u32[]{:S(2)}) collective-permute-start(bf16[1,32,896]{2,1,0:T(8,128)(2,1)S(1)} %bitcast.73), channel_id=1, source_target_pairs={{0,13},{1,12},{2,15},{3,14},{4,9},{5,8},{6,11},{7,10},{8,5},{9,4},... | collective-permute-start | bytes 172040 | tf_op jit(solution)/shard_map/ppermute | solution.py:59
  26.5 12.9 %collective-permute-start.28 = (bf16[1,32,896]{2,1,0:T(8,128)(2,1)S(1)}, bf16[1,32,896]{2,1,0:T(8,128)(2,1)S(1)}, u32[]{:S(2)}, u32[]{:S(2)}) collective-permute-start(bf16[1,32,896]{2,1,0:T(8,128)(2,1)S(1)} %bitcast.72), channel_id=1, source_target_pairs={{0,14},{1,15},{2,12},{3,13},{4,10},{5,11},{6,8},{7,9},{8,6},{9,7},... | collective-permute-start | bytes 172040 | tf_op jit(solution)/shard_map/ppermute | solution.py:59
  31.3 43.8 %slice-start = ((s8[7340032]{0:T(1024)(128)(4,1)}), s8[4194304]{0:T(1024)(128)(4,1)S(1)}, s32[]{:S(2)}) async-start(s8[7340032]{0:T(1024)(128)(4,1)} %bitcast.85), calls=%async_computation | async-start | bytes 8388608
  31.3 39.8 %collective-permute-start.29 = (bf16[1,32,896]{2,1,0:T(8,128)(2,1)S(1)}, bf16[1,32,896]{2,1,0:T(8,128)(2,1)S(1)}, u32[]{:S(2)}, u32[]{:S(2)}) collective-permute-start(bf16[1,32,896]{2,1,0:T(8,128)(2,1)S(1)} %bitcast.71), channel_id=1, source_target_pairs={{0,15},{1,14},{2,13},{3,12},{4,11},{5,10},{6,9},{7,8},{8,7},{9,6},... | collective-permute-start | bytes 172040 | tf_op jit(solution)/shard_map/ppermute | solution.py:59
  34.8 13.7 %collective-permute-start.10 = (bf16[24,2048]{1,0:T(8,128)(2,1)S(1)}, bf16[24,2048]{1,0:T(8,128)(2,1)S(1)}, u32[]{:S(2)}, u32[]{:S(2)}) collective-permute-start(bf16[24,2048]{1,0:T(8,128)(2,1)S(1)} %get-tuple-element.8), channel_id=1, source_target_pairs={{0,8},{1,9},{2,10},{3,11},{4,12},{5,13},{6,14},{7,15},{8,0},{9,1},... | collective-permute-start | bytes 294920 | tf_op jit(solution)/shard_map/ppermute | solution.py:13
  34.8 13.7 %collective-permute-start.11 = (bf16[24,2048]{1,0:T(8,128)(2,1)S(1)}, bf16[24,2048]{1,0:T(8,128)(2,1)S(1)}, u32[]{:S(2)}, u32[]{:S(2)}) collective-permute-start(bf16[24,2048]{1,0:T(8,128)(2,1)S(1)} %get-tuple-element.8), channel_id=1, source_target_pairs={{0,4},{1,5},{2,6},{3,7},{4,0},{5,1},{6,2},{7,3},{8,12},{9,13},{10,... | collective-permute-start | bytes 294920 | tf_op jit(solution)/shard_map/ppermute | solution.py:13
  35.6 15.5 %collective-permute-start.12 = (bf16[24,2048]{1,0:T(8,128)(2,1)S(1)}, bf16[24,2048]{1,0:T(8,128)(2,1)S(1)}, u32[]{:S(2)}, u32[]{:S(2)}) collective-permute-start(bf16[24,2048]{1,0:T(8,128)(2,1)S(1)} %get-tuple-element.8), channel_id=1, source_target_pairs={{0,12},{1,13},{2,14},{3,15},{4,8},{5,9},{6,10},{7,11},{8,4},{9,5},... | collective-permute-start | bytes 294920 | tf_op jit(solution)/shard_map/ppermute | solution.py:13
  39.4 13.4 %collective-permute-start.1 = (bf16[24,2048]{1,0:T(8,128)(2,1)S(1)}, bf16[24,2048]{1,0:T(8,128)(2,1)S(1)}, u32[]{:S(2)}, u32[]{:S(2)}) collective-permute-start(bf16[24,2048]{1,0:T(8,128)(2,1)S(1)} %get-tuple-element.6), channel_id=1, source_target_pairs={{0,8},{1,9},{2,10},{3,11},{4,12},{5,13},{6,14},{7,15},{8,0},{9,1},... | collective-permute-start | bytes 294920 | tf_op jit(solution)/shard_map/ppermute | solution.py:13
  48.5 8.4 %collective-permute-start.2 = (bf16[24,2048]{1,0:T(8,128)(2,1)S(1)}, bf16[24,2048]{1,0:T(8,128)(2,1)S(1)}, u32[]{:S(2)}, u32[]{:S(2)}) collective-permute-start(bf16[24,2048]{1,0:T(8,128)(2,1)S(1)} %get-tuple-element.6), channel_id=1, source_target_pairs={{0,4},{1,5},{2,6},{3,7},{4,0},{5,1},{6,2},{7,3},{8,12},{9,13},{10,... | collective-permute-start | bytes 294920 | tf_op jit(solution)/shard_map/ppermute | solution.py:13
  48.5 8.4 %collective-permute-start.3 = (bf16[24,2048]{1,0:T(8,128)(2,1)S(1)}, bf16[24,2048]{1,0:T(8,128)(2,1)S(1)}, u32[]{:S(2)}, u32[]{:S(2)}) collective-permute-start(bf16[24,2048]{1,0:T(8,128)(2,1)S(1)} %get-tuple-element.6), channel_id=1, source_target_pairs={{0,12},{1,13},{2,14},{3,15},{4,8},{5,9},{6,10},{7,11},{8,4},{9,5},... | collective-permute-start | bytes 294920 | tf_op jit(solution)/shard_map/ppermute | solution.py:13
  51.2 19.4 %collective-permute-start.13 = (bf16[96,2048]{1,0:T(8,128)(2,1)S(1)}, bf16[96,2048]{1,0:T(8,128)(2,1)S(1)}, u32[]{:S(2)}, u32[]{:S(2)}) collective-permute-start(bf16[96,2048]{1,0:T(8,128)(2,1)S(1)} %pad_maximum_fusion.1), channel_id=1, source_target_pairs={{0,2},{1,3},{2,0},{3,1},{4,6},{5,7},{6,4},{7,5},{8,10},{9,11},{10,... | collective-permute-start | bytes 1179656 | tf_op jit(solution)/shard_map/ppermute | solution.py:13
  56.9 13.5 %collective-permute-start.4 = (bf16[96,2048]{1,0:T(8,128)(2,1)S(1)}, bf16[96,2048]{1,0:T(8,128)(2,1)S(1)}, u32[]{:S(2)}, u32[]{:S(2)}) collective-permute-start(bf16[96,2048]{1,0:T(8,128)(2,1)S(1)} %pad_maximum_fusion), channel_id=1, source_target_pairs={{0,2},{1,3},{2,0},{3,1},{4,6},{5,7},{6,4},{7,5},{8,10},{9,11},{10,... | collective-permute-start | bytes 1179656 | tf_op jit(solution)/shard_map/ppermute | solution.py:13
  70.5 2.4 %collective-permute-start.5 = (bf16[192,2048]{1,0:T(8,128)(2,1)S(1)}, bf16[192,2048]{1,0:T(8,128)(2,1)S(1)}, u32[]{:S(2)}, u32[]{:S(2)}) collective-permute-start(bf16[192,2048]{1,0:T(8,128)(2,1)S(1)} %constant_dynamic-update-slice_fusion), channel_id=1, source_target_pairs={{0,1},{1,0},{2,3},{3,2},{4,5},{5,4},{6,7},{7,6},{8,9},{9,8},{10,11... | collective-permute-start | bytes 2359304 | tf_op jit(solution)/shard_map/ppermute | solution.py:13
  70.6 4.5 %collective-permute-start.14 = (bf16[192,2048]{1,0:T(8,128)(2,1)S(1)}, bf16[192,2048]{1,0:T(8,128)(2,1)S(1)}, u32[]{:S(2)}, u32[]{:S(2)}) collective-permute-start(bf16[192,2048]{1,0:T(8,128)(2,1)S(1)} %constant_dynamic-update-slice_fusion.5), channel_id=1, source_target_pairs={{0,1},{1,0},{2,3},{3,2},{4,5},{5,4},{6,7},{7,6},{8,9},{9,8},{10,11... | collective-permute-start | bytes 2359304 | tf_op jit(solution)/shard_map/ppermute | solution.py:13
  71.2 3.9 %slice-start.1 = ((s8[7340032]{0:T(1024)(128)(4,1)}), s8[3145728]{0:T(1024)(128)(4,1)S(1)}, s32[]{:S(2)}) async-start(s8[7340032]{0:T(1024)(128)(4,1)} %bitcast.85), calls=%async_computation.1 | async-start | bytes 6291456
  73.5 3.4 %slice-start.2 = ((s8[7340032]{0:T(1024)(128)(4,1)}), s8[4194304]{0:T(1024)(128)(4,1)S(1)}, s32[]{:S(2)}) async-start(s8[7340032]{0:T(1024)(128)(4,1)} %bitcast.87), calls=%async_computation.2 | async-start | bytes 8388608
  73.5 3.4 %slice-start.3 = ((s8[7340032]{0:T(1024)(128)(4,1)}), s8[3145728]{0:T(1024)(128)(4,1)S(1)}, s32[]{:S(2)}) async-start(s8[7340032]{0:T(1024)(128)(4,1)} %bitcast.87), calls=%async_computation.3 | async-start | bytes 6291456
  73.5 6.1 %collective-permute-start.6 = (f32[96,32]{0,1:T(8,128)S(1)}, f32[96,32]{0,1:T(8,128)S(1)}, u32[]{:S(2)}, u32[]{:S(2)}) collective-permute-start(f32[96,32]{0,1:T(8,128)S(1)} %get-tuple-element.34), channel_id=1, source_target_pairs={{0,2},{1,3},{2,0},{3,1},{4,6},{5,7},{6,4},{7,5},{8,10},{9,11},{10,... | collective-permute-start | bytes 36872 | tf_op jit(solution)/shard_map/ppermute | solution.py:13
  79.5 4.2 %collective-permute-start.30 = (f32[192,256]{1,0:T(8,128)S(1)}, f32[192,256]{1,0:T(8,128)S(1)}, u32[]{:S(2)}, u32[]{:S(2)}) collective-permute-start(f32[192,256]{1,0:T(8,128)S(1)} %convolution_add_fusion), channel_id=1, source_target_pairs={{0,1},{1,0},{2,3},{3,2},{4,5},{5,4},{6,7},{7,6},{8,9},{9,8},{10,11... | collective-permute-start | bytes 589832 | tf_op jit(solution)/shard_map/ppermute | solution.py:13
  79.7 3.9 %collective-permute-start.7 = (f32[48,64]{0,1:T(8,128)S(1)}, f32[48,64]{0,1:T(8,128)S(1)}, u32[]{:S(2)}, u32[]{:S(2)}) collective-permute-start(f32[48,64]{0,1:T(8,128)S(1)} %get-tuple-element.32), channel_id=1, source_target_pairs={{0,4},{1,5},{2,6},{3,7},{4,0},{5,1},{6,2},{7,3},{8,12},{9,13},{10,... | collective-permute-start | bytes 36872 | tf_op jit(solution)/shard_map/ppermute | solution.py:13
  84.0 4.7 %collective-permute-start.31 = (f32[96,256]{1,0:T(8,128)S(1)}, f32[96,256]{1,0:T(8,128)S(1)}, u32[]{:S(2)}, u32[]{:S(2)}) collective-permute-start(f32[96,256]{1,0:T(8,128)S(1)} %slice.100), channel_id=1, source_target_pairs={{0,2},{1,3},{2,0},{3,1},{4,6},{5,7},{6,4},{7,5},{8,10},{9,11},{10,... | collective-permute-start | bytes 294920 | tf_op jit(solution)/shard_map/ppermute | solution.py:13
  88.7 4.2 %collective-permute-start.32 = (f32[48,256]{1,0:T(8,128)S(1)}, f32[48,256]{1,0:T(8,128)S(1)}, u32[]{:S(2)}, u32[]{:S(2)}) collective-permute-start(f32[48,256]{1,0:T(8,128)S(1)} %slice.102), channel_id=1, source_target_pairs={{0,4},{1,5},{2,6},{3,7},{4,0},{5,1},{6,2},{7,3},{8,12},{9,13},{10,... | collective-permute-start | bytes 147464 | tf_op jit(solution)/shard_map/ppermute | solution.py:13
  89.6 4.9 %collective-permute-start.8 = (f32[24,128]{1,0:T(8,128)S(1)}, f32[24,128]{1,0:T(8,128)S(1)}, u32[]{:S(2)}, u32[]{:S(2)}) collective-permute-start(f32[24,128]{1,0:T(8,128)S(1)} %get-tuple-element.36), channel_id=1, source_target_pairs={{0,8},{1,9},{2,10},{3,11},{4,12},{5,13},{6,14},{7,15},{8,0},{9,1},... | collective-permute-start | bytes 36872 | tf_op jit(solution)/shard_map/ppermute | solution.py:13
  92.9 4.8 %collective-permute-start.33 = (f32[24,256]{1,0:T(8,128)S(1)}, f32[24,256]{1,0:T(8,128)S(1)}, u32[]{:S(2)}, u32[]{:S(2)}) collective-permute-start(f32[24,256]{1,0:T(8,128)S(1)} %slice.104), channel_id=1, source_target_pairs={{0,8},{1,9},{2,10},{3,11},{4,12},{5,13},{6,14},{7,15},{8,0},{9,1},... | collective-permute-start | bytes 73736 | tf_op jit(solution)/shard_map/ppermute | solution.py:13
  98.2 1.2 %collective-permute-start.34 = (f32[12,16]{0,1:T(8,128)S(1)}, f32[12,16]{0,1:T(8,128)S(1)}, u32[]{:S(2)}, u32[]{:S(2)}) collective-permute-start(f32[12,16]{0,1:T(8,128)S(1)} %slice_select_fusion), channel_id=1, source_target_pairs={{0,1},{1,0},{2,3},{3,2},{4,5},{5,4},{6,7},{7,6},{8,9},{9,8},{10,11... | collective-permute-start | bytes 2312 | tf_op jit(solution)/shard_map/ppermute | solution.py:13
